TPU v7x, 32 devices: a whole 2x2x4 slice. The times are simulated.
32 devices in a mesh: blk: 16 (over z, y, core), rows: 2 (over x).
Axes of the slice: x: 2, y: 2, z: 4, core: 2. Of those that a mesh axis runs over, the one named last changes fastest.
Arguments:
- tokens: bfloat16 [64, 8192], P(('blk', 'rows')), may hold values from -60 to 60
- norm_gain: float32 [8192], replicated, may hold values from 0.1 to 1.9
- gate_weight: bfloat16 [8192, 4096], P(None, 'blk'), may hold values from -0.09375 to 0.09375
- up_weight: bfloat16 [8192, 4096], P(None, 'blk'), may hold values from -0.09375 to 0.09375
- down_weight: bfloat16 [4096, 8192], P('blk'), may hold values from -0.125 to 0.125
- gate_mask: int32 [64, 32], P(None, 'blk'), may hold values from 0 to 1, as said below
- up_mask: int32 [64, 32], P(None, 'blk'), may hold values from 0 to 1, as said below
- down_mask: int32 [32, 64], P('blk'), may hold values 0 or 1
Outputs:
- ffn_out: bfloat16 [64, 8192], P(('blk', 'rows'))
Inputs may be any that keep to these rules, and one draw needn't show every extreme that they name: Each column of gate_mask (64 block flags) has between 16 and 48 ones, and some column has exactly 48. Each column of up_mask (64 block flags) has between 16 and 48 ones, and some column has exactly 48.
All inputs are finite; a program needn't handle non-finite values. No bound on the sum of `down_mask` on one device may be relied on, other than what follows from the above.
Results may differ from a plain program's by a relative error of at most 0.0065.
Values may be sent and summed in bfloat16 or wider, within the bound.
A program may use at most 128 MiB of HBM per device.

v0:
```python
import jax
import jax.numpy as jnp
from jax import lax
from jax.sharding import PartitionSpec as P


def mask_blocks(weight, flags):
    height, width = weight.shape
    down_n = flags.shape[0]
    across_n = flags.shape[1]
    shaped = weight.reshape(down_n, height // down_n, across_n, width // across_n)
    return (shaped * flags.astype(weight.dtype)[:, None, :, None]).reshape(height, width)


def local(tokens, norm_gain, gate_weight, up_weight, down_weight, gate_mask, up_mask, down_mask):
    wide_tok = tokens.astype(jnp.float32)
    scale_inv = lax.rsqrt(jnp.mean(wide_tok * wide_tok, axis=-1, keepdims=True) + 1e-05)
    normed = (wide_tok * scale_inv * norm_gain).astype(jnp.bfloat16)
    gate_own, up_own, down_own = (gate_weight, up_weight, down_weight)
    gate_flags, up_flags, down_flags = (gate_mask, up_mask, down_mask)
    gate_kept = mask_blocks(gate_own, gate_flags)
    up_kept = mask_blocks(up_own, up_flags)
    down_kept = mask_blocks(down_own, down_flags)
    piece = lax.all_gather(normed, "blk", axis=0, tiled=True)
    gate = jnp.dot(piece, gate_kept, preferred_element_type=jnp.float32)
    up_val = jnp.dot(piece, up_kept, preferred_element_type=jnp.float32)
    hidden = (jax.nn.silu(gate) * up_val).astype(jnp.bfloat16)
    summed = lax.psum_scatter(
        jnp.dot(hidden, down_kept, preferred_element_type=jnp.float32),
        "blk",
        scatter_dimension=0,
        tiled=True,
    )
    return summed.astype(jnp.bfloat16)


def solution(mesh):
    return jax.shard_map(
        local,
        mesh=mesh,
        in_specs=(
            P(("blk", "rows"), None),
            P(),
            P(None, "blk"),
            P(None, "blk"),
            P("blk", None),
            P(None, "blk"),
            P(None, "blk"),
            P("blk", None),
        ),
        out_specs=P(("blk", "rows"), None),
        check_vma=False,
    )
```

profile of v0, /device:TPU:0, one launch (start us, length us, event | category | flops | bytes accessed | tf_op | source)
XLA Modules:
  0.0 120.5 jit_solution(15726329001007055776)
XLA Ops:
  0.0 0.9 fusion.8
  0.9 0.9 fusion.16
  1.8 24.6 %all-gather = bf16[16,2,8192]{2,1,0:T(2,128)(2,1)S(1)} all-gather(bf16[1,2,8192]{2,1,0:T(2,128)(2,1)S(1)} %fusion.16), channel_id=1, replica_groups=mesh['blk'=16,'rows'=2] {'blk'}, dimensions={0}, use_global_device_ids=true | all-gather | bytes 557056 | tf_op jit(solution)/shard_map/all_gather | solution.py:24
  26.4 0.2 reshape.22
  26.6 0.7 convert_element_type.23
  27.3 0.1 copy.11
  27.4 0.0 copy-start
  27.4 2.2 %mul.64 = bf16[64,128,2,128]{3,2,1,0:T(2,128)(2,1)S(1)} broadcast(bf16[64,2]{1,0:T(8,128)(2,1)S(1)} %copy.11), dimensions={0,2} | broadcast | bytes 4194560 | tf_op jit(solution)/shard_map/mul | solution.py:12
  29.7 0.0 copy-done
  29.7 0.0 copy-start.1
  29.7 0.9 fusion.4
  30.6 0.0 copy-done.1
  30.6 0.0 copy-start.2
  30.6 0.1 copy.12
  30.8 4.2 %mul.68 = bf16[64,128,2,128]{3,2,1,0:T(2,128)(2,1)} broadcast(bf16[64,2]{1,0:T(8,128)(2,1)S(1)} %copy.12), dimensions={0,2} | broadcast | bytes 4194560 | tf_op jit(solution)/shard_map/mul | solution.py:12
  35.0 0.0 copy-done.2
  35.0 3.1 %mul.72 = bf16[2,128,64,128]{3,2,1,0:T(8,128)(2,1)} broadcast(bf16[2,64]{1,0:T(2,128)(2,1)S(1)} %convert_element_type.26), dimensions={0,2} | broadcast | bytes 4194560 | tf_op jit(solution)/shard_map/mul | solution.py:12
  38.0 0.0 copy-start.3
  38.0 11.1 %fusion = f32[32,8192]{1,0:T(8,128)S(1)} fusion(bf16[256,8192]{1,0:T(8,128)(2,1)} %param.12, bf16[32,8,64,128]{3,2,1,0:T(8,128)(2,1)} %bitcast.28, bf16[32,8192]{1,0:T(8,128)(2,1)S(1)} %reshape.22, bf16[8192,256]{1,0:T(8,128)(2,1)} %param.11, bf16[1024,8,2,128]{3,2,1,0:T(2,128)(2,1)} %bitcast.27, f32[32,256]{1,0:T(8,128)S(1)} %fusion.4), kind=kOutput, calls=%fused_computation.1 | convolution fusion | flops 272678912 | bytes 18382848 | tf_op jit(solution)/shard_map/dot_general | solution.py:29
  49.1 69.5 %all-reduce.2 = bf16[32,8192]{1,0:T(8,128)(2,1)S(1)} all-reduce(f32[32,8192]{1,0:T(8,128)S(1)} %fusion), channel_id=2, replica_groups=mesh['blk'=16,'rows'=2] {'blk'}, use_global_device_ids=true, to_apply=%region_1.2.clone | all-reduce | flops 262144 | bytes 1572864
  118.6 0.0 copy-done.3
  118.6 0.6 dynamic-slice
  119.9 0.7 dynamic-slice_convert_fusion
  (3 shorter events, 0.0 us)
Async XLA Ops:
  27.4 2.2 %copy-start = (bf16[8192,256]{1,0:T(8,128)(2,1)S(1)}, bf16[8192,256]{1,0:T(8,128)(2,1)}, u32[]{:S(2)}) copy-start(bf16[8192,256]{1,0:T(8,128)(2,1)} %param.10) | copy-start | bytes 12582916
  29.7 0.9 copy-start.1
  30.6 4.3 %copy-start.2 = (s32[2,64]{1,0:T(2,128)S(1)}, s32[2,64]{1,0:T(2,128)}, u32[]{:S(2)}) copy-start(s32[2,64]{1,0:T(2,128)} %param.15) | copy-start | bytes 1540
  38.0 80.6 %copy-start.3 = (u32[32]{0:T(128)S(1)}, u32[32]{0:T(128)}, u32[]{:S(2)}) copy-start(u32[32]{0:T(128)} %constant.16) | copy-start | bytes 388
where the time goes:
time: 121 us
  blocking collectives  94.1 us (78%)
  matrix products  12 us (10%)
  local copies, waits for them, and re-layouts  11.2 us (9%)
  other arithmetic  2.52 us (2%)
    unnamed x1, blocking collectives  69.5 us
    all_gather x1, blocking collectives, local(): piece = lax.all_gather(normed, 'blk', axis=0, tiled=True)  24.6 us
    dot_general x1, matrix products, local(): jnp.dot(hidden, down_kept, preferred_element_type=jnp.float32)  11.1 us
    mul x3, local copies, waits for them, and re-layouts, mask_blocks(): shaped * flags.astype(weight.dtype)[:, None, :, None]  9.48 us

commit v1 on v0

v1 whole, which is shorter than its diff:
```python
import functools

import jax
import jax.numpy as jnp
from jax import lax
from jax.experimental import pallas as pl
from jax.experimental.pallas import tpu as pltpu
from jax.sharding import PartitionSpec as P

MESH = pl.DeviceIdType.MESH
F32 = jnp.float32
BF16 = jnp.bfloat16
LANES = 128
CUT = 1024
GROUP = 16


def permutation(to_tokens):
    size = GROUP * 16
    row = lax.broadcasted_iota(jnp.int32, (size, size), 0)
    col = lax.broadcasted_iota(jnp.int32, (size, size), 1)
    if not to_tokens:
        row, col = col, row
    block, device, token = row >> 5, (row & 31) >> 1, row & 1
    return jnp.where(device * 16 + block * 2 + token == col, 1.0, 0.0).astype(BF16)


def kernel(
    nblk,
    tok_ref,
    gain_ref,
    gm_ref,
    um_ref,
    dm_ref,
    wg_hbm,
    wu_hbm,
    wd_hbm,
    out_ref,
    wg,
    wu,
    wd,
    wide,
    slabs,
    x,
    swap_out,
    swap_in,
    rs_out,
    rs_in,
    fin_out,
    fin_in,
    w_sem,
    ag_send,
    fw_send,
    ag_recv,
    swap_send,
    swap_recv,
    rs_send,
    rs_recv,
    fin_send,
    fin_recv,
):
    nchips = nblk // 2
    feats = wg.shape[0]
    hid = wg.shape[1]
    blocks = feats // LANES
    cuts = feats // CUT
    half_cuts = cuts // 2
    rows_half = blocks
    groups = nblk // GROUP
    me = lax.axis_index("blk")
    chip, core = me // 2, me % 2
    sib = chip * 2 + (1 - core)

    def peer(o):
        return lax.rem(chip + o, nchips)

    loads = []
    for n in range(4):
        r = feats // 4
        rs = pl.ds(n * r, r)
        loads.append(
            (
                pltpu.make_async_copy(wg_hbm.at[rs], wg.at[rs], w_sem.at[0, n]),
                pltpu.make_async_copy(wu_hbm.at[rs], wu.at[rs], w_sem.at[1, n]),
            )
        )
    down_loads = []
    for n in range(4):
        r = feats // 4
        cs = pl.ds(n * r, r)
        down_loads.append(pltpu.make_async_copy(wd_hbm.at[:, cs], wd.at[:, cs], w_sem.at[2, n]))
    for a, b in loads:
        a.start()
        b.start()
    for a in down_loads:
        a.start()

    barrier = pltpu.get_barrier_semaphore()
    pl.semaphore_signal(barrier, inc=1, device_id={"blk": sib}, device_id_type=MESH)

    def greet(o, c):
        pl.semaphore_signal(barrier, inc=1, device_id={"blk": peer(o) * 2 + core}, device_id_type=MESH)
        return c

    lax.fori_loop(1, nchips, greet, 0)

    tok = tok_ref[...].astype(F32)
    inv = lax.rsqrt(jnp.mean(tok * tok, axis=-1, keepdims=True) + 1e-05)
    normed = tok * inv * gain_ref[...]
    for b in range(blocks):
        wide[pl.ds(2 * b, 2), :] = normed[:, b * LANES : (b + 1) * LANES]
    slabs[me] = wide[...].astype(BF16)

    pl.semaphore_wait(barrier, nchips)

    def ag_copy(src, dev, send):
        return pltpu.make_async_remote_copy(
            src_ref=slabs.at[src],
            dst_ref=slabs.at[src],
            send_sem=send,
            recv_sem=ag_recv.at[src],
            device_id={"blk": dev},
            device_id_type=MESH,
        )

    def send_all(o, c):
        ag_copy(me, peer(o) * 2 + core, ag_send.at[o]).start()
        return c

    lax.fori_loop(1, nchips, send_all, 0)
    ag_copy(me, sib, ag_send.at[0]).start()

    def flagged(w, flag):
        keep = jnp.broadcast_to(flag.astype(F32), (16, LANES)).astype(BF16)
        return (w.reshape(8, 16, LANES) * keep[None]).reshape(LANES, LANES)

    per = blocks // 4
    for n in range(4):
        loads[n][0].wait()
        loads[n][1].wait()

        def mask_in(i, c):
            i = n * per + i
            rs = pl.ds(pl.multiple_of(i * LANES, LANES), LANES)
            for j in range(hid // LANES):
                cs = pl.ds(j * LANES, LANES)
                wg[rs, cs] = flagged(wg[rs, cs], gm_ref[i, j])
                wu[rs, cs] = flagged(wu[rs, cs], um_ref[i, j])
            return c

        lax.fori_loop(0, per, mask_in, 0)

    def forward(o, c):
        src = lax.rem(chip + nchips - o, nchips) * 2 + core
        ag_copy(src, sib, fw_send.at[o]).wait_recv()
        ag_copy(src, sib, fw_send.at[o]).start()
        return c

    lax.fori_loop(1, nchips, forward, 0)

    for n in range(4):
        down_loads[n].wait()

        def mask_down(i, c):
            i = n * per + i
            cs = pl.ds(pl.multiple_of(i * LANES, LANES), LANES)
            for j in range(hid // LANES):
                rs = pl.ds(j * LANES, LANES)
                wd[rs, cs] = flagged(wd[rs, cs], dm_ref[j, i])
            return c

        lax.fori_loop(0, per, mask_down, 0)

    def arrived(o, c):
        src = lax.rem(chip + nchips - o, nchips) * 2 + (1 - core)
        ag_copy(src, sib, fw_send.at[0]).wait_recv()
        return c

    lax.fori_loop(0, nchips, arrived, 0)

    to_tokens = permutation(True)
    gate = jnp.zeros((2 * nblk, hid), F32)
    up = jnp.zeros((2 * nblk, hid), F32)
    for n in range(cuts):
        for g in range(groups):
            part = slabs[pl.ds(g * GROUP, GROUP), pl.ds(n * 16, 16), :].reshape(GROUP * 16, LANES)
            turned = jnp.dot(to_tokens, part, preferred_element_type=F32).astype(BF16)
            for b in range(8):
                x[pl.ds(g * 32, 32), pl.ds(b * LANES, LANES)] = turned[b * 32 : (b + 1) * 32]
        rs = pl.ds(n * CUT, CUT)
        gate = gate + jnp.dot(x[...], wg[rs, :], preferred_element_type=F32)
        up = up + jnp.dot(x[...], wu[rs, :], preferred_element_type=F32)
    hidden = (gate / (1.0 + jnp.exp(-gate)) * up).astype(BF16)

    def swap_copy(n):
        cs = pl.ds(n * CUT, CUT)
        return pltpu.make_async_remote_copy(
            src_ref=swap_out.at[:, cs],
            dst_ref=swap_in.at[:, cs],
            send_sem=swap_send.at[n],
            recv_sem=swap_recv.at[n],
            device_id={"blk": sib},
            device_id_type=MESH,
        )

    for n in range(half_cuts):
        at = pl.multiple_of(((1 - core) * half_cuts + n) * CUT, CUT)
        part = jnp.dot(hidden, wd[:, pl.ds(at, CUT)], preferred_element_type=F32)
        swap_out[:, pl.ds(n * CUT, CUT)] = part.astype(BF16)
        swap_copy(n).start()

    to_slabs = permutation(False)
    for n in range(half_cuts):
        at = pl.multiple_of((core * half_cuts + n) * CUT, CUT)
        part = jnp.dot(hidden, wd[:, pl.ds(at, CUT)], preferred_element_type=F32)
        swap_copy(n).wait_recv()
        both = (part + swap_in[:, pl.ds(n * CUT, CUT)].astype(F32)).astype(BF16)
        for g in range(groups):
            mine = both[g * 32 : (g + 1) * 32]
            stacked = jnp.concatenate([mine[:, b * LANES : (b + 1) * LANES] for b in range(8)], axis=0)
            turned = jnp.dot(to_slabs, stacked, preferred_element_type=F32).astype(BF16)
            rs_out[pl.ds(g * GROUP // 2, GROUP // 2), :, pl.ds(n * 16, 16), :] = turned.reshape(
                GROUP // 2, 2, 16, LANES
            )

    def rs_copy(src, dst, o, dev):
        return pltpu.make_async_remote_copy(
            src_ref=rs_out.at[src],
            dst_ref=rs_in.at[dst],
            send_sem=rs_send.at[o],
            recv_sem=rs_recv.at[dst],
            device_id={"blk": dev},
            device_id_type=MESH,
        )

    def rs_start(o, c):
        to = peer(o)
        rs_copy(to, chip, o, to * 2 + core).start()
        return c

    lax.fori_loop(1, nchips, rs_start, 0)

    def rs_add(o, total):
        src = lax.rem(chip + nchips - o, nchips)
        rs_copy(src, src, o, src * 2 + core).wait_recv()
        return total + rs_in[src].astype(F32)

    total = lax.fori_loop(1, nchips, rs_add, rs_out[chip].astype(F32))
    fin_out[...] = total.astype(BF16)
    fin = pltpu.make_async_remote_copy(
        src_ref=fin_out.at[1 - core],
        dst_ref=fin_in,
        send_sem=fin_send,
        recv_sem=fin_recv,
        device_id={"blk": sib},
        device_id_type=MESH,
    )
    fin.start()
    out_ref[core] = fin_out[core]

    def drain(o, c):
        ag_copy(me, sib, ag_send.at[o]).wait_send()
        ag_copy(me, sib, fw_send.at[o]).wait_send()
        rs_copy(chip, chip, o, sib).wait_send()
        return c

    lax.fori_loop(1, nchips, drain, 0)
    ag_copy(me, sib, ag_send.at[0]).wait_send()
    for n in range(half_cuts):
        swap_copy(n).wait_send()
    fin.wait()
    out_ref[1 - core] = fin_in[...]


def local(nblk, tokens, norm_gain, gate_weight, up_weight, down_weight, gate_mask, up_mask, down_mask):
    own, feats = tokens.shape
    hid = gate_weight.shape[1]
    blocks = feats // LANES
    half = feats // 2
    nchips = nblk // 2
    cuts = half // CUT
    vmem = pl.BlockSpec(memory_space=pltpu.VMEM)
    smem = pl.BlockSpec(memory_space=pltpu.SMEM)
    anyw = pl.BlockSpec(memory_space=pl.ANY)
    dma = pltpu.SemaphoreType.DMA
    out = pl.pallas_call(
        functools.partial(kernel, nblk),
        out_shape=jax.ShapeDtypeStruct((2, blocks, LANES), BF16),
        in_specs=[vmem, vmem, smem, smem, smem, anyw, anyw, anyw],
        out_specs=vmem,
        scratch_shapes=[
            pltpu.VMEM((feats, hid), BF16),
            pltpu.VMEM((feats, hid), BF16),
            pltpu.VMEM((hid, feats), BF16),
            pltpu.VMEM((2 * blocks, LANES), F32),
            pltpu.VMEM((nblk, 2 * blocks, LANES), BF16),
            pltpu.VMEM((2 * nblk, CUT), BF16),
            pltpu.VMEM((2 * nblk, half), BF16),
            pltpu.VMEM((2 * nblk, half), BF16),
            pltpu.VMEM((nchips, 2, blocks, LANES), BF16),
            pltpu.VMEM((nchips, 2, blocks, LANES), BF16),
            pltpu.VMEM((2, blocks, LANES), BF16),
            pltpu.VMEM((blocks, LANES), BF16),
            dma((3, 4)),
            dma((nchips,)),
            dma((nchips,)),
            dma((nblk,)),
            dma((cuts,)),
            dma((cuts,)),
            dma((nchips,)),
            dma((nchips,)),
            dma,
            dma,
        ],
        compiler_params=pltpu.CompilerParams(
            collective_id=0, has_side_effects=True, vmem_limit_bytes=50 * 1024 * 1024
        ),
    )(
        tokens,
        norm_gain.reshape(1, feats),
        gate_mask,
        up_mask,
        down_mask,
        gate_weight,
        up_weight,
        down_weight,
    )
    return out.reshape(blocks, 2, LANES).transpose(1, 0, 2).reshape(own, feats)


def solution(mesh):
    return jax.shard_map(
        functools.partial(local, mesh.shape["blk"]),
        mesh=mesh,
        in_specs=(
            P(("blk", "rows"), None),
            P(),
            P(None, "blk"),
            P(None, "blk"),
            P("blk", None),
            P(None, "blk"),
            P(None, "blk"),
            P("blk", None),
        ),
        out_specs=P(("blk", "rows"), None),
        check_vma=False,
    )
```

time: 121 us -> 33.1 us (0.27)
  blocking collectives: 94.1 us -> 0 us
  Pallas kernels: 0 us -> 28.3 us
  matrix products: 12 us -> 0 us
  local copies, waits for them, and re-layouts: 11.2 us -> 4.35 us
  other arithmetic: 2.52 us -> 0 us
    unnamed x1 -> x0, blocking collectives: 69.5 us -> none
    pallas_call x0 -> x1, Pallas kernels: none -> 28.3 us  [local(): pl.pallas_call(functools.partial(kernel, nblk), out_shape=jax.ShapeDtypeS...]
    all_gather x1 -> x0, blocking collectives: 24.6 us -> none  [local(): piece = lax.all_gather(normed, 'blk', axis=0, tiled=True)]
    dot_general x2 -> x0, matrix products: 12 us -> none  [the longest x1 11.1 us: local(): jnp.dot(hidden, down_kept, preferred_element_type=jnp.float32)]
    mul x3 -> x0, local copies, waits for them, and re-layouts: 9.48 us -> none  [mask_blocks(): shaped * flags.astype(weight.dtype)[:, None, :, None]]
    unnamed x10 -> x9, local copies, waits for them, and re-layouts: 0.8 us -> 4.35 us
where the time goes in v1:
time: 33.1 us; the launch traced here: 32.7 us
  Pallas kernels  28.3 us (85%)
  local copies, waits for them, and re-layouts  4.35 us (13%)
    pallas_call x1, Pallas kernels, local(): pl.pallas_call(functools.partial(kernel, nblk), out_shape=jax.ShapeDtypeS...  28.3 us
    unnamed x9, local copies, waits for them, and re-layouts  4.35 us

profile of v1, /device:TPU:0, one launch (start us, length us, event | category | flops | bytes accessed | tf_op | source)
XLA Modules:
  0.0 32.7 jit_solution(5990640137391132193)
XLA Ops:
  0.0 0.8 %copy.9.gm_ref = s32[64,2]{1,0:T(8,128)S(1)} copy(s32[64,2]{0,1:T(2,128)} %param.13) | data formatting | bytes 1024 | tf_op args[5]
  0.8 0.8 %copy.10.um_ref = s32[64,2]{1,0:T(8,128)S(1)} copy(s32[64,2]{0,1:T(2,128)} %param.14) | data formatting | bytes 1024 | tf_op args[6]
  1.5 0.0 copy-start
  1.5 0.8 %copy-done = bf16[2,8192]{1,0:T(2,128)(2,1)S(1)} copy-done((bf16[2,8192]{1,0:T(2,128)(2,1)S(1)}, bf16[2,8192]{1,0:T(2,128)(2,1)}, u32[]{:S(2)}) %copy-start) | copy-done | bytes 32792
  2.3 0.0 copy-start.1
  2.3 0.8 %copy-done.1 = f32[8192]{0:T(1024)S(1)} copy-done((f32[8192]{0:T(1024)S(1)}, f32[8192]{0:T(1024)}, u32[]{:S(2)}) %copy-start.1) | copy-done | bytes 32792
  3.1 0.0 copy-start.2
  3.1 0.7 %copy-done.2 = s32[2,64]{1,0:T(2,128)S(1)} copy-done((s32[2,64]{1,0:T(2,128)S(1)}, s32[2,64]{1,0:T(2,128)}, u32[]{:S(2)}) %copy-start.2) | copy-done | bytes 536
  3.7 28.3 %shard_map.82 = bf16[2,64,128]{2,1,0:T(8,128)(2,1)S(1)} custom-call(bf16[2,8192]{1,0:T(2,128)(2,1)S(1)} %copy-done, f32[1,8192]{1,0:T(1,128)S(1)} %bitcast.7, s32[64,2]{1,0:T(8,128)S(1)} %copy.9.gm_ref, s32[64,2]{1,0:T(8,128)S(1)} %copy.10.um_ref, s32[2,64]{1,0:T(2,128)S(1)} %copy-done.2, bf16[8192,256]{1,0:T(8,128)(2,1)} %wg_hbm.1, ...), custom_call_target="tpu_custom_call" | custom-call | tf_op jit(solution)/shard_map/pallas_call | solution.py:286
  32.0 0.6 %copy.13 = bf16[2,8192]{1,0:T(2,128)(2,1)} copy(bf16[2,8192]{1,0:T(2,128)(2,1)S(1)} %bitcast.6) | data formatting | bytes 65536
Async XLA Ops:
  1.5 0.8 %copy-start = (bf16[2,8192]{1,0:T(2,128)(2,1)S(1)}, bf16[2,8192]{1,0:T(2,128)(2,1)}, u32[]{:S(2)}) copy-start(bf16[2,8192]{1,0:T(2,128)(2,1)} %tok_ref.1) | copy-start | bytes 98308
  2.3 0.8 %copy-start.1 = (f32[8192]{0:T(1024)S(1)}, f32[8192]{0:T(1024)}, u32[]{:S(2)}) copy-start(f32[8192]{0:T(1024)} %param.9) | copy-start | bytes 98308
  3.1 0.7 %copy-start.2 = (s32[2,64]{1,0:T(2,128)S(1)}, s32[2,64]{1,0:T(2,128)}, u32[]{:S(2)}) copy-start(s32[2,64]{1,0:T(2,128)} %dm_ref.1) | copy-start | bytes 1540

commit v2 on v1

--- a/solution.py
+++ b/solution.py
@@ -27,15 +27,20 @@
 
 def kernel(
     nblk,
+    tok_hbm,
+    gain_hbm,
+    gm_hbm,
+    um_hbm,
+    dm_hbm,
+    wg_hbm,
+    wu_hbm,
+    wd_hbm,
+    out_ref,
     tok_ref,
     gain_ref,
     gm_ref,
     um_ref,
     dm_ref,
-    wg_hbm,
-    wu_hbm,
-    wd_hbm,
-    out_ref,
     wg,
     wu,
     wd,
@@ -48,8 +53,10 @@
     rs_in,
     fin_out,
     fin_in,
+    s_sem,
     w_sem,
     ag_send,
+    by_send,
     fw_send,
     ag_recv,
     swap_send,
@@ -74,6 +81,21 @@
     def peer(o):
         return lax.rem(chip + o, nchips)
 
+    smalls = [
+        pltpu.make_async_copy(a, b, s_sem.at[n])
+        for n, (a, b) in enumerate(
+            (
+                (tok_hbm, tok_ref),
+                (gain_hbm, gain_ref),
+                (gm_hbm, gm_ref),
+                (um_hbm, um_ref),
+                (dm_hbm, dm_ref),
+            )
+        )
+    ]
+    for a in smalls:
+        a.start()
+
     loads = []
     for n in range(4):
         r = feats // 4
@@ -104,6 +126,8 @@
 
     lax.fori_loop(1, nchips, greet, 0)
 
+    smalls[0].wait()
+    smalls[1].wait()
     tok = tok_ref[...].astype(F32)
     inv = lax.rsqrt(jnp.mean(tok * tok, axis=-1, keepdims=True) + 1e-05)
     normed = tok * inv * gain_ref[...]
@@ -123,12 +147,35 @@
             device_id_type=MESH,
         )
 
+    pairs = nchips // 2
+    pair, side = chip // 2, chip % 2
+    beside = (pair * 2 + (1 - side)) * 2 + core
+
+    def slab_of(o, s, c):
+        return (lax.rem(pair + pairs - o, pairs) * 2 + s) * 2 + c
+
     def send_all(o, c):
-        ag_copy(me, peer(o) * 2 + core, ag_send.at[o]).start()
-        return c
-
-    lax.fori_loop(1, nchips, send_all, 0)
-    ag_copy(me, sib, ag_send.at[0]).start()
+        ag_copy(me, (lax.rem(pair + o, pairs) * 2 + side) * 2 + core, ag_send.at[o]).start()
+        return c
+
+    lax.fori_loop(1, pairs, send_all, 0)
+    ag_copy(me, beside, by_send.at[0]).start()
+    ag_copy(me, sib, fw_send.at[0, 0]).start()
+    for a in smalls[2:]:
+        a.wait()
+
+    def forward_both(o, c):
+        src = slab_of(o, side, core)
+        ag_copy(src, sib, fw_send.at[0, o]).wait_recv()
+        ag_copy(src, beside, by_send.at[o]).start()
+        ag_copy(src, sib, fw_send.at[0, o]).start()
+        return c
+
+    def forward_last(o, c):
+        src = slab_of(o, 1 - side, core)
+        ag_copy(src, sib, fw_send.at[1, o]).wait_recv()
+        ag_copy(src, sib, fw_send.at[1, o]).start()
+        return c
 
     def flagged(w, flag):
         keep = jnp.broadcast_to(flag.astype(F32), (16, LANES)).astype(BF16)
@@ -144,19 +191,12 @@
             rs = pl.ds(pl.multiple_of(i * LANES, LANES), LANES)
             for j in range(hid // LANES):
                 cs = pl.ds(j * LANES, LANES)
-                wg[rs, cs] = flagged(wg[rs, cs], gm_ref[i, j])
-                wu[rs, cs] = flagged(wu[rs, cs], um_ref[i, j])
+                wg[rs, cs] = flagged(wg[rs, cs], gm_ref[j, i])
+                wu[rs, cs] = flagged(wu[rs, cs], um_ref[j, i])
             return c
 
         lax.fori_loop(0, per, mask_in, 0)
-
-    def forward(o, c):
-        src = lax.rem(chip + nchips - o, nchips) * 2 + core
-        ag_copy(src, sib, fw_send.at[o]).wait_recv()
-        ag_copy(src, sib, fw_send.at[o]).start()
-        return c
-
-    lax.fori_loop(1, nchips, forward, 0)
+        lax.fori_loop(1 + (pairs - 1) * n // 4, 1 + (pairs - 1) * (n + 1) // 4, forward_both, 0)
 
     for n in range(4):
         down_loads[n].wait()
@@ -170,10 +210,11 @@
             return c
 
         lax.fori_loop(0, per, mask_down, 0)
+        lax.fori_loop(pairs * n // 4, pairs * (n + 1) // 4, forward_last, 0)
 
     def arrived(o, c):
         src = lax.rem(chip + nchips - o, nchips) * 2 + (1 - core)
-        ag_copy(src, sib, fw_send.at[0]).wait_recv()
+        ag_copy(src, sib, fw_send.at[0, 0]).wait_recv()
         return c
 
     lax.fori_loop(0, nchips, arrived, 0)
@@ -209,6 +250,17 @@
         swap_out[:, pl.ds(n * CUT, CUT)] = part.astype(BF16)
         swap_copy(n).start()
 
+    def rs_copy(src, dst, o, dev, n):
+        rows = pl.ds(n * 16, 16)
+        return pltpu.make_async_remote_copy(
+            src_ref=rs_out.at[src, :, rows],
+            dst_ref=rs_in.at[dst, :, rows],
+            send_sem=rs_send.at[o, n],
+            recv_sem=rs_recv.at[dst, n],
+            device_id={"blk": dev},
+            device_id_type=MESH,
+        )
+
     to_slabs = permutation(False)
     for n in range(half_cuts):
         at = pl.multiple_of((core * half_cuts + n) * CUT, CUT)
@@ -223,26 +275,17 @@
                 GROUP // 2, 2, 16, LANES
             )
 
-    def rs_copy(src, dst, o, dev):
-        return pltpu.make_async_remote_copy(
-            src_ref=rs_out.at[src],
-            dst_ref=rs_in.at[dst],
-            send_sem=rs_send.at[o],
-            recv_sem=rs_recv.at[dst],
-            device_id={"blk": dev},
-            device_id_type=MESH,
-        )
-
-    def rs_start(o, c):
-        to = peer(o)
-        rs_copy(to, chip, o, to * 2 + core).start()
-        return c
-
-    lax.fori_loop(1, nchips, rs_start, 0)
+        def rs_start(o, c):
+            to = peer(o)
+            rs_copy(to, chip, o, to * 2 + core, n).start()
+            return c
+
+        lax.fori_loop(1, nchips, rs_start, 0)
 
     def rs_add(o, total):
         src = lax.rem(chip + nchips - o, nchips)
-        rs_copy(src, src, o, src * 2 + core).wait_recv()
+        for n in range(half_cuts):
+            rs_copy(src, src, o, src * 2 + core, n).wait_recv()
         return total + rs_in[src].astype(F32)
 
     total = lax.fori_loop(1, nchips, rs_add, rs_out[chip].astype(F32))
@@ -258,14 +301,24 @@
     fin.start()
     out_ref[core] = fin_out[core]
 
-    def drain(o, c):
+    def drain_own(o, c):
         ag_copy(me, sib, ag_send.at[o]).wait_send()
-        ag_copy(me, sib, fw_send.at[o]).wait_send()
-        rs_copy(chip, chip, o, sib).wait_send()
-        return c
-
-    lax.fori_loop(1, nchips, drain, 0)
-    ag_copy(me, sib, ag_send.at[0]).wait_send()
+        return c
+
+    def drain_forwards(o, c):
+        ag_copy(me, sib, by_send.at[o]).wait_send()
+        ag_copy(me, sib, fw_send.at[0, o]).wait_send()
+        ag_copy(me, sib, fw_send.at[1, o]).wait_send()
+        return c
+
+    def drain_sums(o, c):
+        for n in range(half_cuts):
+            rs_copy(chip, chip, o, sib, n).wait_send()
+        return c
+
+    lax.fori_loop(1, pairs, drain_own, 0)
+    lax.fori_loop(0, pairs, drain_forwards, 0)
+    lax.fori_loop(1, nchips, drain_sums, 0)
     for n in range(half_cuts):
         swap_copy(n).wait_send()
     fin.wait()
@@ -280,15 +333,20 @@
     nchips = nblk // 2
     cuts = half // CUT
     vmem = pl.BlockSpec(memory_space=pltpu.VMEM)
-    smem = pl.BlockSpec(memory_space=pltpu.SMEM)
+    held = pl.BlockSpec(memory_space=pltpu.HBM)
     anyw = pl.BlockSpec(memory_space=pl.ANY)
     dma = pltpu.SemaphoreType.DMA
     out = pl.pallas_call(
         functools.partial(kernel, nblk),
         out_shape=jax.ShapeDtypeStruct((2, blocks, LANES), BF16),
-        in_specs=[vmem, vmem, smem, smem, smem, anyw, anyw, anyw],
+        in_specs=[held] * 5 + [anyw] * 3,
         out_specs=vmem,
         scratch_shapes=[
+            pltpu.VMEM((own, feats), BF16),
+            pltpu.VMEM((1, feats), F32),
+            pltpu.SMEM((hid // LANES, blocks), jnp.int32),
+            pltpu.SMEM((hid // LANES, blocks), jnp.int32),
+            pltpu.SMEM((hid // LANES, blocks), jnp.int32),
             pltpu.VMEM((feats, hid), BF16),
             pltpu.VMEM((feats, hid), BF16),
             pltpu.VMEM((hid, feats), BF16),
@@ -301,25 +359,27 @@
             pltpu.VMEM((nchips, 2, blocks, LANES), BF16),
             pltpu.VMEM((2, blocks, LANES), BF16),
             pltpu.VMEM((blocks, LANES), BF16),
+            dma((5,)),
             dma((3, 4)),
-            dma((nchips,)),
-            dma((nchips,)),
+            dma((nchips // 2,)),
+            dma((nchips // 2,)),
+            dma((2, nchips // 2)),
             dma((nblk,)),
             dma((cuts,)),
             dma((cuts,)),
-            dma((nchips,)),
-            dma((nchips,)),
+            dma((nchips, cuts)),
+            dma((nchips, cuts)),
             dma,
             dma,
         ],
         compiler_params=pltpu.CompilerParams(
-            collective_id=0, has_side_effects=True, vmem_limit_bytes=50 * 1024 * 1024
+            collective_id=0, has_side_effects=True, vmem_limit_bytes=64 * 1024 * 1024 - 65536
         ),
     )(
         tokens,
         norm_gain.reshape(1, feats),
-        gate_mask,
-        up_mask,
+        gate_mask.T,
+        up_mask.T,
         down_mask,
         gate_weight,
         up_weight,

time: 33.1 us -> 31 us (0.937)
  local copies, waits for them, and re-layouts: 4.35 us -> 1.4 us
  Pallas kernels: 28.3 us -> 29.4 us
    unnamed x9 -> x1, local copies, waits for them, and re-layouts: 4.35 us -> 1.4 us
    pallas_call x1, Pallas kernels: 28.3 us -> 29.4 us  [local(): pl.pallas_call(functools.partial(kernel, nblk), out_shape=jax.ShapeDtypeS...]
where the time goes in v2:
time: 31 us; the launch traced here: 30.8 us
  Pallas kernels  29.4 us (95%)
  local copies, waits for them, and re-layouts  1.4 us (5%)
    pallas_call x1, Pallas kernels, local(): pl.pallas_call(functools.partial(kernel, nblk), out_shape=jax.ShapeDtypeS...  29.4 us
    unnamed x1, local copies, waits for them, and re-layouts  1.4 us

profile of v2, /device:TPU:0, one launch (start us, length us, event | category | flops | bytes accessed | tf_op | source)
XLA Modules:
  0.0 30.8 jit_solution(7901826060303015509)
XLA Ops:
  0.0 29.4 %shard_map.82 = bf16[2,64,128]{2,1,0:T(8,128)(2,1)} custom-call(bf16[2,8192]{1,0:T(2,128)(2,1)} %tok_hbm.1, f32[1,8192]{1,0:T(1,128)} %bitcast.9, s32[2,64]{1,0:T(2,128)} %bitcast.10, s32[2,64]{1,0:T(2,128)} %bitcast.11, s32[2,64]{1,0:T(2,128)} %dm_hbm.1, bf16[8192,256]{1,0:T(8,128)(2,1)} %wg_hbm.1, bf16[8192,256]{1,0:T(8,128)(2,1)} %wu_hbm.1, ...), custom_call_target="tpu_custom_call" | custom-call | tf_op jit(solution)/shard_map/pallas_call | solution.py:339
  29.4 1.4 %copy.11 = bf16[2,8192]{1,0:T(2,128)(2,1)} copy(bf16[2,8192]{1,0:T(2,128)(2,1)} %bitcast.8) | data formatting | bytes 65536

commit v3 on v2

--- a/solution.py
+++ b/solution.py
@@ -195,7 +195,7 @@
                 wu[rs, cs] = flagged(wu[rs, cs], um_ref[j, i])
             return c
 
-        lax.fori_loop(0, per, mask_in, 0)
+        lax.fori_loop(0, per, mask_in, 0, unroll=4)
         lax.fori_loop(1 + (pairs - 1) * n // 4, 1 + (pairs - 1) * (n + 1) // 4, forward_both, 0)
 
     for n in range(4):
@@ -209,7 +209,7 @@
                 wd[rs, cs] = flagged(wd[rs, cs], dm_ref[j, i])
             return c
 
-        lax.fori_loop(0, per, mask_down, 0)
+        lax.fori_loop(0, per, mask_down, 0, unroll=4)
         lax.fori_loop(pairs * n // 4, pairs * (n + 1) // 4, forward_last, 0)
 
     def arrived(o, c):

time: 31 us -> 31 us (level)
  no operation moved by 1% of the time
where the time goes in v3:
time: 31 us; the launch traced here: 30.8 us
  Pallas kernels  29.4 us (95%)
  local copies, waits for them, and re-layouts  1.4 us (5%)
    pallas_call x1, Pallas kernels, local(): pl.pallas_call(functools.partial(kernel, nblk), out_shape=jax.ShapeDtypeS...  29.4 us
    unnamed x1, local copies, waits for them, and re-layouts  1.4 us

profile of v3, /device:TPU:0, one launch (start us, length us, event | category | flops | bytes accessed | tf_op | source)
XLA Modules:
  0.0 30.8 jit_solution(15980272427633840589)
XLA Ops:
  0.0 29.4 %shard_map.82 = bf16[2,64,128]{2,1,0:T(8,128)(2,1)} custom-call(bf16[2,8192]{1,0:T(2,128)(2,1)} %tok_hbm.1, f32[1,8192]{1,0:T(1,128)} %bitcast.9, s32[2,64]{1,0:T(2,128)} %bitcast.10, s32[2,64]{1,0:T(2,128)} %bitcast.11, s32[2,64]{1,0:T(2,128)} %dm_hbm.1, bf16[8192,256]{1,0:T(8,128)(2,1)} %wg_hbm.1, bf16[8192,256]{1,0:T(8,128)(2,1)} %wu_hbm.1, ...), custom_call_target="tpu_custom_call" | custom-call | tf_op jit(solution)/shard_map/pallas_call | solution.py:339
  29.4 1.4 %copy.11 = bf16[2,8192]{1,0:T(2,128)(2,1)} copy(bf16[2,8192]{1,0:T(2,128)(2,1)} %bitcast.8) | data formatting | bytes 65536
